TPU v7x, 256 devices: a whole 4x4x8 slice. The times are simulated.
256 devices in a mesh: tile: 32 (over z, y), lev: 8 (over x, core).
Axes of the slice: x: 4, y: 4, z: 8, core: 2. Of those that a mesh axis runs over, the one named last changes fastest.
Arguments:
- members: bfloat16 [32, 65536, 128], P('lev', 'tile'), may hold values from -4 to 4
- obs_operator: bfloat16 [8, 2048, 4, 128, 128], P('lev', 'tile'), as said below
- col_level: int32 [8, 2048, 4], P('lev', 'tile'), may hold values from 0 to 3
- col_block: int32 [8, 2048, 4], P('lev', 'tile'), may hold values from 0 to 19, as said below
- obs_count: int32 [2048], P(('tile', 'lev')), may hold values from 1 to 128, as said below
- obs_values: float32 [2048, 128], P(('tile', 'lev')), may hold values from -60 to 60
- obs_weight: float32 [2048, 128], P(('tile', 'lev')), may hold values from 0.01 to 0.18
Outputs:
- analysed: bfloat16 [32, 65536, 128], P('lev', 'tile')
- transform: float32 [128, 128], replicated
Inputs may be any that keep to these rules, and one draw needn't show every extreme that they name: `col_block`: for the observation block in position i of its tile (i < 64), every column block lies within 2 of i * 16 // 64 + 2, and never names a block outside the grid. `obs_count`: the first block of every tile uses all 128 rows. `obs_operator`: entries lie within 4 / sqrt(8192) of zero.
All inputs are finite; a program needn't handle non-finite values.
Results may differ from a plain program's by a relative error of at most 0.0076.
Values may be sent and summed in bfloat16 or wider, within the bound.
No kernel may reach another device: no remote copies, remote signals or barrier semaphores. Data moves between devices by JAX's collectives and lax.ppermute only.
A program may use at most 128 MiB of HBM per device.

v0:
```python
import math

import jax
import jax.numpy as jnp
from jax import lax
from jax.sharding import PartitionSpec as P

HALO = 2


def with_halo(value, sides, width):
    for axis, dim in sides:
        count, length = (lax.axis_size(axis), value.shape[dim])
        up = [(i, (i + 1) % count) for i in range(count - 1)]
        down = [(j, i) for i, j in up]
        last = lax.slice_in_dim(value, length - width, length, axis=dim)
        first = lax.slice_in_dim(value, 0, width, axis=dim)
        before = lax.ppermute(last, axis, up)
        after = lax.ppermute(first, axis, down)
        value = jnp.concatenate([before, value, after], axis=dim)
    return value


def shards(members, obs_operator, col_level, col_block, obs_count, obs_values, obs_weight):
    highest = lax.Precision.HIGHEST
    lev_local, cells_local, ensemble = members.shape
    block_size = obs_operator.shape[-1]
    rim_cells = HALO * block_size
    padded = with_halo(members, (("tile", 1),), rim_cells)
    window_blocks = padded.shape[1] // block_size
    column_blocks = padded.reshape(lev_local, window_blocks, block_size, ensemble).reshape(
        lev_local * window_blocks, block_size, ensemble
    )
    operator_blocks = obs_operator[0]
    flat_index = col_level[0] * window_blocks + col_block[0]
    live_rows = (jnp.arange(block_size, dtype=jnp.int32)[None, :] < obs_count[:, None]).astype(
        jnp.float32
    )
    weight_local = obs_weight * live_rows
    chosen = column_blocks[flat_index]
    observed = lax.psum_scatter(
        jnp.einsum("okij,okjm->oim", operator_blocks, chosen, preferred_element_type=jnp.float32),
        "lev",
        scatter_dimension=0,
        tiled=True,
    )
    weight, values_used = (weight_local, obs_values)
    mean_obs = jnp.sum(observed, axis=2) / ensemble
    row_scale = weight / math.sqrt(ensemble - 1)
    spread = ((observed - mean_obs[:, :, None]) * row_scale[:, :, None]).reshape(-1, ensemble)
    innovation = ((values_used - mean_obs) * weight).reshape(-1)
    gram_local = jnp.dot(spread.T, spread, precision=highest, preferred_element_type=jnp.float32)
    pull_local = jnp.dot(innovation, spread, precision=highest, preferred_element_type=jnp.float32)
    identity = jnp.eye(ensemble, dtype=jnp.float32)
    gram, pull = lax.psum((gram_local, pull_local), ("tile", "lev"))
    lower = jnp.linalg.cholesky(identity + gram)
    inverse = lax.linalg.triangular_solve(lower, identity, left_side=True, lower=True)
    shift_weights = jnp.dot(inverse.T, jnp.dot(inverse, pull, precision=highest), precision=highest)
    transform = shift_weights[:, None] / math.sqrt(ensemble - 1) + inverse.T
    transform_bf = transform.astype(jnp.bfloat16)
    row_mean = jnp.sum(members, axis=2, dtype=jnp.float32) / ensemble
    anomalies = (members.astype(jnp.float32) - row_mean[:, :, None]).astype(jnp.bfloat16)
    moved = jnp.dot(
        anomalies.reshape(-1, ensemble), transform_bf, preferred_element_type=jnp.float32
    )
    analysed = (row_mean[:, :, None] + moved.reshape(lev_local, cells_local, ensemble)).astype(
        jnp.bfloat16
    )
    return (analysed, transform)


def solution(mesh):
    placed = (
        P("lev", "tile", None),
        P("lev", "tile", None, None, None),
        P("lev", "tile", None),
        P("lev", "tile", None),
        P(("tile", "lev")),
        P(("tile", "lev"), None),
        P(("tile", "lev"), None),
    )
    return jax.shard_map(
        shards, mesh=mesh, in_specs=placed, out_specs=(P("lev", "tile", None), P()), check_vma=False
    )
```

profile of v0, /device:TPU:1, one launch (start us, length us, event | category | flops | bytes accessed | tf_op | source)
XLA Modules:
  0.0 369.6 jit_solution(11171952963979726350)
XLA Ops:
  7.2 1.1 fusion.23
  8.3 4.0 %collective-permute-start = (bf16[4,256,128]{2,1,0:T(8,128)(2,1)S(1)}, bf16[4,256,128]{2,1,0:T(8,128)(2,1)S(1)}, u32[]{:S(2)}, u32[]{:S(2)}) collective-permute-start(bf16[4,256,128]{2,1,0:T(8,128)(2,1)S(1)} %get-tuple-element.6), channel_id=1, source_target_pairs={{0,8},{8,16},{16,24},{24,32},{32,40},{40,48},{48,56},{56,64},{64,7... | collective-permute-start | bytes 786440 | tf_op jit(solution)/shard_map/ppermute | solution.py:18
  12.3 1.3 collective-permute-start.1
  13.6 0.7 compare_select_fusion
  14.6 2.7 collective-permute-done
  17.3 3.8 %collective-permute-done.1 = bf16[4,256,128]{2,1,0:T(8,128)(2,1)S(1)} collective-permute-done((bf16[4,256,128]{2,1,0:T(8,128)(2,1)S(1)}, bf16[4,256,128]{2,1,0:T(8,128)(2,1)S(1)}, u32[]{:S(2)}, u32[]{:S(2)}) %collective-permute-start.1) | collective-permute-done | bytes 262176 | tf_op jit(solution)/shard_map/ppermute | solution.py:19
  21.1 1.8 pad_maximum_fusion
  22.9 8.6 %gather_fusion = bf16[256,128,128]{2,1,0:T(8,128)(2,1)} fusion(bf16[80,128,128]{2,1,0:T(8,128)(2,1)S(1)} %bitcast.54, s32[1024]{0:T(1024)S(1)} %pad_clamp_fusion), kind=kCustom, calls=%fused_computation | custom fusion | bytes 16778240 | tf_op jit(solution)/shard_map/gather | solution.py:40
  31.5 10.1 %fusion.3 = f32[64,128,128]{1,2,0:T(8,128)} fusion(bf16[64,4,128,128]{3,2,1,0:T(8,128)(2,1)} %bitcast.55, bf16[1,64,4,128,128]{4,3,2,1,0:T(8,128)(2,1)} %param.8), kind=kOutput, calls=%fused_computation.8 | convolution fusion | flops 1073741824 | bytes 20971520 | tf_op jit(solution)/shard_map/okij,okjm->oim/dot_general | solution.py:42
  41.7 1.5 copy-done
  43.9 41.4 %reduce-scatter.2.cloned.1.call-done = f32[8,128,128]{1,2,0:T(8,128)} async-done(((f32[64,128,128]{1,2,0:T(8,128)}), f32[8,128,128]{1,2,0:T(8,128)}) %reduce-scatter.2.cloned.1.call-update) | async-done | bytes 524304 | tf_op jit(solution)/shard_map/reduce_scatter | solution.py:41
  85.3 1.1 reduce_sum.19
  86.5 2.5 convolution_bitcast_fusion
  89.0 1.6 convolution_bitcast_fusion.3
  90.5 79.5 %psum.15 = f32[128]{0:T(128)S(1)} all-reduce(f32[128]{0:T(128)S(1)} %convolution_bitcast_fusion.3), channel_id=1, replica_groups=mesh['tile'=32,'lev'=8] {'tile','lev'}, use_global_device_ids=true, to_apply=%region_6.7 | all-reduce | flops 128 | bytes 1024 | tf_op jit(solution)/shard_map/psum | solution.py:55
  170.0 161.5 %all-reduce.2.cloned.1.call-done = f32[128,128]{1,0:T(8,128)} async-done(((f32[128,128]{1,0:T(8,128)}), f32[128,128]{1,0:T(8,128)}) %all-reduce.2.cloned.1.call-update) | async-done | bytes 65552 | tf_op jit(solution)/shard_map/psum | solution.py:55
  331.5 0.9 convert_add_fusion
  332.4 0.9 fusion.17
  333.3 11.7 %cholesky.18 = f32[128,128]{1,0:T(8,128)S(1)} custom-call(f32[128,128]{1,0:T(8,128)S(1)} %fusion.17), custom_call_target="Cholesky" | custom-call | tf_op jit(solution)/shard_map/jit(cholesky)/cholesky | solution.py:56
  345.0 0.6 compare_reduce_fusion
  345.7 0.7 fusion.13
  346.3 9.8 %custom-call.6 = f32[1,128,128]{1,2,0:T(8,128)S(1)} custom-call(f32[1,128,128]{2,1,0:T(8,128)S(1)} %fusion.13), custom_call_target="InvertDiagBlocksLowerTriangular" | custom-call | tf_op jit(solution)/shard_map/triangular_solve | solution.py:57
  356.8 0.7 copy.19
  357.5 5.3 %add_convert_fusion = bf16[4,2048,128]{2,1,0:T(8,128)(2,1)} fusion(bf16[4,2048,128]{2,1,0:T(8,128)(2,1)S(1)} %copy-done, f32[4,2048]{1,0:T(4,128)S(1)} %broadcast_multiply_fusion, f32[128,128]{0,1:T(8,128)S(1)} %bitcast_add_fusion), kind=kOutput, calls=%fused_computation.6 | convolution fusion | flops 273694720 | bytes 4292608 | tf_op jit(solution)/shard_map/dot_general | solution.py:63
  (23 shorter events, 1.8 us)
Async XLA Ops:
  7.2 78.2 %reduce-scatter.2.cloned.1.call-start = ((), (), s32[]{:S(2)}) async-start(), calls=%async_computation.1 | async-start | bytes 4718592 | tf_op jit(solution)/shard_map/reduce_scatter | solution.py:41
  8.3 9.0 %collective-permute-start = (bf16[4,256,128]{2,1,0:T(8,128)(2,1)S(1)}, bf16[4,256,128]{2,1,0:T(8,128)(2,1)S(1)}, u32[]{:S(2)}, u32[]{:S(2)}) collective-permute-start(bf16[4,256,128]{2,1,0:T(8,128)(2,1)S(1)} %get-tuple-element.6), channel_id=1, source_target_pairs={{0,8},{8,16},{16,24},{24,32},{32,40},{40,48},{48,56},{56,64},{64,7... | collective-permute-start | bytes 786440 | tf_op jit(solution)/shard_map/ppermute | solution.py:18
  12.3 8.8 %collective-permute-start.1 = (bf16[4,256,128]{2,1,0:T(8,128)(2,1)S(1)}, bf16[4,256,128]{2,1,0:T(8,128)(2,1)S(1)}, u32[]{:S(2)}, u32[]{:S(2)}) collective-permute-start(bf16[4,256,128]{2,1,0:T(8,128)(2,1)S(1)} %get-tuple-element.7), channel_id=1, source_target_pairs={{8,0},{16,8},{24,16},{32,24},{40,32},{48,40},{56,48},{64,56},{72,6... | collective-permute-start | bytes 786440 | tf_op jit(solution)/shard_map/ppermute | solution.py:19
  41.6 1.6 copy-start
  41.6 44.8 %copy-start.1 = (f32[8,128]{1,0:T(8,128)S(1)}, f32[8,128]{1,0:T(8,128)}, u32[]{:S(2)}) copy-start(f32[8,128]{1,0:T(8,128)} %param.12) | copy-start | bytes 12292
  41.6 44.8 %copy-start.2 = (f32[8,128]{1,0:T(8,128)S(1)}, f32[8,128]{1,0:T(8,128)}, u32[]{:S(2)}) copy-start(f32[8,128]{1,0:T(8,128)} %param.13) | copy-start | bytes 12292
  41.6 44.8 %copy-start.3 = (s32[8]{0:T(128)S(1)}, s32[8]{0:T(128)}, u32[]{:S(2)}) copy-start(s32[8]{0:T(128)} %param.11) | copy-start | bytes 100
  41.7 289.8 %all-reduce.2.cloned.1.call-start = ((), (), s32[]{:S(2)}) async-start(), calls=%async_computation.2 | async-start | bytes 131072 | tf_op jit(solution)/shard_map/psum | solution.py:55
Sparse Core Ops, SparseCore 0:
  41.8 43.4 reduce-scatter.1
  91.4 240.0 all-reduce.1
where the time goes:
time: 370 us
  waiting for transfers between devices  209 us (56%)
  blocking collectives  79.5 us (21%)
  other arithmetic  28.9 us (8%)
  matrix products  20 us (5%)
  between operations  14.2 us (4%)
  local copies, waits for them, and re-layouts  12.2 us (3%)
  starting transfers between devices  5.42 us (1%)
    psum x1, waiting for transfers between devices, shards(): gram, pull = lax.psum((gram_local, pull_local), ('tile', 'lev'))  161 us
    psum x1, blocking collectives, shards(): gram, pull = lax.psum((gram_local, pull_local), ('tile', 'lev'))  79.5 us
    reduce_scatter x1, waiting for transfers between devices, shards(): lax.psum_scatter(jnp.einsum('okij,okjm->oim', operator_blocks, chosen, pr...  41.4 us
    another operation x3, other arithmetic, shards(): lower = jnp.linalg.cholesky(identity + gram)  12.4 us
    another operation x2, other arithmetic, shards(): lax.linalg.triangular_solve(lower, identity, left_side=True, lower=True)  10.5 us
    dot_general x1, matrix products, shards(): jnp.einsum('okij,okjm->oim', operator_blocks, chosen, preferred_element_t...  10.1 us
    gather x1, local copies, waits for them, and re-layouts, shards(): chosen = column_blocks[flat_index]  8.62 us
  transfers between devices with their start and end apart: 4, of which 4 were waited for; matrix products, arithmetic and copies ran while one was open for 1% of the time, Pallas kernels for 0%

commit v1 on v0

v1 whole, which is shorter than its diff:
```python
import functools
import math

import jax
import jax.numpy as jnp
from jax import lax
from jax.experimental import pallas as pl
from jax.experimental.pallas import tpu as pltpu
from jax.sharding import PartitionSpec as P

BLK = 128
HALO = 2
RIM = HALO * BLK
NNZ = 4
LEVS = 4
CELLS = 2048
OWN = 8
DATA = OWN * BLK
TAIL = 32
ROWS = DATA + TAIL
NEAR = 4 * BLK
EDGE = NEAR + RIM
BF, F32 = jnp.bfloat16, jnp.float32
HIGHEST = lax.Precision.HIGHEST
VMEM = pltpu.VMEM
SMEM = pltpu.SMEM
HBM = pltpu.HBM


def other_core(value):
    return lax.ppermute(value, "lev", [(i, i ^ 1) for i in range(8)])


def x_shift(value, step):
    return lax.ppermute(value, "lev", [(i, (i + 2 * step) % 8) for i in range(8)])


def place(z, y, x, core):
    return (z * 4 + y) * 8 + x * 2 + core


PLANES = [[place(z, y, x, c) for y in range(4) for x in range(4)] for z in range(8) for c in range(2)]
LINES = [[place(z, y, x, c) for z in range(8)] for y in range(4) for x in range(4) for c in range(2)]


def group_sum(value, groups):
    copies = jnp.broadcast_to(value[None], (len(groups[0]),) + value.shape)
    came = lax.all_to_all(copies, ("tile", "lev"), 0, 0, axis_index_groups=groups)
    return jnp.sum(came, axis=0)


def split_means(mean):
    high = mean.astype(BF).astype(F32)
    rest = mean - high
    mid = rest.astype(BF).astype(F32)
    low = rest - mid
    return jnp.concatenate([high, mid, low, jnp.zeros_like(low)], axis=0).astype(BF)


def join_means(tail):
    parts = tail.astype(F32)
    return (parts[0:8] + parts[8:16]) + parts[16:24]


def observe_owner(owner, at_ref, op_ref, window_ref, length, base, out_ref):
    lane = lax.broadcasted_iota(jnp.int32, (BLK, BLK), 1)
    means = jnp.zeros((BLK, BLK), F32)

    def product(j):
        o = owner * OWN + j
        rows = []
        for k in range(NNZ):
            at = (at_ref[0, k, o] // 32) * length + (at_ref[0, k, o] % 32 - base) * BLK
            rows.append(window_ref[pl.ds(pl.multiple_of(at, BLK), BLK), :])
        return jnp.dot(
            jnp.concatenate([op_ref[0, j, k] for k in range(NNZ)], axis=1),
            jnp.concatenate(rows, axis=0),
            preferred_element_type=F32,
        )

    ahead = 1
    parts = [product(j) for j in range(ahead)]
    for j in range(OWN):
        if j + ahead < OWN:
            parts.append(product(j + ahead))
        part = parts[j]
        mean = jnp.sum(part, axis=1, keepdims=True) * (1.0 / BLK)
        out_ref[j * BLK : (j + 1) * BLK, :] = (part - mean).astype(BF)
        means = jnp.where(lane == j, mean, means)
    out_ref[DATA:ROWS, :] = split_means(jnp.transpose(means)[0:OWN])


CHUNKS_IN = 3


def inner_kernel(
    core_ref, at_ref, op_hbm, members_hbm,
    send_ref, keep_ref, edge_ref, rim_ref, held, members_ref, sem, edge_sem, rim_sem, members_sem,
):
    core = core_ref[0]

    def blocks(owner):
        return op_hbm.at[:, pl.ds(owner * OWN, OWN)]

    def owner_of(n):
        parity = 1 - core if n < CHUNKS_IN else core
        return 2 * (n % CHUNKS_IN) + 2 - parity

    loads = [pltpu.make_async_copy(members_hbm, members_ref, members_sem)]
    loads[0].start(priority=1)
    for n in range(2 * CHUNKS_IN):
        loads.append(pltpu.make_async_copy(blocks(owner_of(n)), held.at[n], sem.at[n]))
        loads[-1].start(priority=n % 2)
    edges = [pltpu.make_async_copy(blocks(7 * n), edge_ref.at[n], edge_sem.at[n]) for n in range(2)]
    for n in range(2):
        for v in range(LEVS):
            cells = members_hbm.at[pl.ds(v * CELLS + n * (CELLS - NEAR), NEAR)]
            edges.append(pltpu.make_async_copy(cells, rim_ref.at[n, v], rim_sem.at[n, v]))
    for n, copy in enumerate(edges):
        copy.start(priority=n % 2)
    loads[0].wait()
    for n in range(2 * CHUNKS_IN):
        loads[n + 1].wait()
        out = send_ref if n < CHUNKS_IN else keep_ref
        observe_owner(
            owner_of(n), at_ref, held.at[n], members_ref, CELLS, HALO, out.at[n % CHUNKS_IN]
        )
    for copy in edges:
        copy.wait()


def inner_blocks(core, places, operator, members):
    out = jax.ShapeDtypeStruct((CHUNKS_IN, ROWS, BLK), BF)
    return pl.pallas_call(
        inner_kernel,
        in_specs=[pl.BlockSpec(memory_space=SMEM)] * 2 + [pl.BlockSpec(memory_space=HBM)] * 2,
        out_specs=[pl.BlockSpec(memory_space=VMEM)] * 4,
        out_shape=[
            out,
            out,
            jax.ShapeDtypeStruct((2, 1, OWN, NNZ, BLK, BLK), BF),
            jax.ShapeDtypeStruct((2, LEVS, NEAR, BLK), BF),
        ],
        scratch_shapes=[
            pltpu.VMEM((2 * CHUNKS_IN, 1, OWN, NNZ, BLK, BLK), BF),
            pltpu.VMEM((LEVS * CELLS, BLK), BF),
            pltpu.SemaphoreType.DMA((2 * CHUNKS_IN,)),
            pltpu.SemaphoreType.DMA((2,)),
            pltpu.SemaphoreType.DMA((2, LEVS)),
            pltpu.SemaphoreType.DMA,
        ],
        compiler_params=pltpu.CompilerParams(vmem_limit_bytes=46 * 2**20),
        cost_estimate=pl.CostEstimate(flops=1_000_000, bytes_accessed=2**16, transcendentals=0),
        name="observe_inner",
    )(core, places, operator, members)


def outer_kernel(
    core_ref, at_ref, edge_ref, rim_ref, before_ref, after_ref, send_ref, keep_ref, low, high
):
    for v in range(LEVS):
        low[v * EDGE : v * EDGE + RIM, :] = before_ref[v]
        low[v * EDGE + RIM : (v + 1) * EDGE, :] = rim_ref[0, v]
        high[v * EDGE : (v + 1) * EDGE - RIM, :] = rim_ref[1, v]
        high[(v + 1) * EDGE - RIM : (v + 1) * EDGE, :] = after_ref[v]

    def run(low_out, high_out):
        observe_owner(0, at_ref, edge_ref.at[0], low, EDGE, 0, low_out)
        observe_owner(7, at_ref, edge_ref.at[1], high, EDGE, 14, high_out)

    @pl.when(core_ref[0] == 0)
    def _():
        run(keep_ref, send_ref)

    @pl.when(core_ref[0] == 1)
    def _():
        run(send_ref, keep_ref)


def outer_blocks(core, places, edge, rim, before, after):
    out = jax.ShapeDtypeStruct((ROWS, BLK), BF)
    return pl.pallas_call(
        outer_kernel,
        in_specs=[pl.BlockSpec(memory_space=SMEM)] * 2 + [pl.BlockSpec(memory_space=VMEM)] * 4,
        out_specs=[pl.BlockSpec(memory_space=VMEM)] * 2,
        out_shape=[out, out],
        scratch_shapes=[pltpu.VMEM((LEVS * EDGE, BLK), BF)] * 2,
        compiler_params=pltpu.CompilerParams(vmem_limit_bytes=32 * 2**20),
        cost_estimate=pl.CostEstimate(flops=270_000_000, bytes_accessed=4 * 2**20, transcendentals=0),
        name="observe_outer",
    )(core, places, edge, rim, before, after)


def pair_kernel(core_ref, x_ref, came_ref, keep_ref, came_edge, keep_edge, *outs):
    core = core_ref[0]

    def add(a_ref, b_ref, out_ref):
        out_ref[0:DATA, :] = (a_ref[0:DATA, :].astype(F32) + b_ref[0:DATA, :].astype(F32)).astype(BF)
        out_ref[DATA:ROWS, :] = split_means(join_means(a_ref[DATA:ROWS, :]) + join_means(b_ref[DATA:ROWS, :]))

    for step in range(4):
        x = lax.rem(x_ref[0] + step, 4)

        @pl.when(x == 3 * core)
        def _():
            add(came_edge, keep_edge, outs[step])

        @pl.when(x != 3 * core)
        def _():
            at = jnp.clip(x - 1 + core, 0, CHUNKS_IN - 1)
            add(came_ref.at[at], keep_ref.at[at], outs[step])


def pair_sum(core, x, came, keep, came_edge, keep_edge):
    out = jax.ShapeDtypeStruct((ROWS, BLK), BF)
    return pl.pallas_call(
        pair_kernel,
        in_specs=[pl.BlockSpec(memory_space=SMEM)] * 2 + [pl.BlockSpec(memory_space=VMEM)] * 4,
        out_specs=[pl.BlockSpec(memory_space=VMEM)] * 4,
        out_shape=[out] * 4,
        compiler_params=pltpu.CompilerParams(vmem_limit_bytes=32 * 2**20),
        name="pair_sum",
    )(core, x, came, keep, came_edge, keep_edge)


HALF = BLK // 2


def pack(gram, pull):
    row = lax.broadcasted_iota(jnp.int32, (HALF, BLK), 0)
    lane = lax.broadcasted_iota(jnp.int32, (HALF, BLK), 1)
    upper, lower = gram[0:HALF], gram[HALF:BLK]
    mixed = jnp.where(lane <= row, upper, pltpu.roll(lower, HALF, 1))
    diagonal = jnp.sum(jnp.where(lane == row + HALF, lower, 0.0), axis=0, keepdims=True)
    quarter = HALF // 2
    left = lax.broadcasted_iota(jnp.int32, (quarter, BLK), 1) < HALF
    first = lax.broadcasted_iota(jnp.int32, (8, BLK), 0) == 0

    def fold(square, extra):
        body = jnp.where(left, square[0:quarter], pltpu.roll(square[quarter:HALF], HALF, 1))
        return jnp.concatenate([body, jnp.where(first, extra, 0.0)], axis=0)

    return fold(lower, pull), fold(mixed, diagonal)


def unpack(zero, one):
    row = lax.broadcasted_iota(jnp.int32, (HALF, BLK), 0)
    lane = lax.broadcasted_iota(jnp.int32, (HALF, BLK), 1)
    quarter = HALF // 2
    pull = zero[quarter : quarter + 1]
    diagonal = one[quarter : quarter + 1]

    def unfold(body):
        return jnp.concatenate([body, pltpu.roll(body, HALF, 1)], axis=0)

    corner = unfold(zero[0:quarter])
    mixed = unfold(one[0:quarter])
    above = jnp.where((lane > row) & (lane < HALF), mixed, 0.0)
    top = jnp.where(lane <= row, mixed, 0.0)
    bottom = jnp.where(lane < HALF, corner, 0.0)
    strict = jnp.concatenate(
        [jnp.where(lane < row, mixed, 0.0), bottom + pltpu.roll(above, HALF, 1)], axis=0
    )
    middle = jnp.where(lane == row + HALF, diagonal, 0.0)
    full = jnp.concatenate([top, bottom + middle + pltpu.roll(above, HALF, 1)], axis=0)
    return full + jnp.transpose(strict), pull


def gram_kernel(
    core_ref, count_ref, a_ref, b_ref, c_ref, d_ref, values_ref, weight_ref, send_ref, keep_ref
):
    parts = (a_ref, b_ref, c_ref, d_ref)
    mean = sum(join_means(ref[DATA:ROWS, :]) for ref in parts)
    row = lax.broadcasted_iota(jnp.int32, (OWN, BLK), 0)
    lane = lax.broadcasted_iota(jnp.int32, (OWN, BLK), 1)
    count = jnp.zeros((OWN, BLK), jnp.int32)
    for j in range(OWN):
        count = jnp.where(row == j, count_ref[j], count)
    weight = jnp.where(lane < count, weight_ref[...], 0.0)
    innovation = (values_ref[...] - mean) * weight
    scale = weight * (1.0 / math.sqrt(BLK - 1))
    columns = jnp.transpose(
        jnp.concatenate([scale, innovation, jnp.zeros((BLK - 2 * OWN, BLK), F32)], axis=0)
    )
    gram = jnp.zeros((BLK, BLK), F32)
    pull = jnp.zeros((1, BLK), F32)
    for j in range(OWN):
        at = slice(j * BLK, (j + 1) * BLK)
        seen = sum(ref[at, :].astype(F32) for ref in parts)
        spread = seen * columns[:, j : j + 1]
        gram += lax.dot_general(
            spread, spread, (((0,), (0,)), ((), ())), precision=HIGHEST, preferred_element_type=F32
        )
        pull += jnp.sum(spread * columns[:, OWN + j : OWN + j + 1], axis=0, keepdims=True)
    core = core_ref[0]
    zero, one = pack(gram, pull)
    keep_ref[...] = jnp.where(core == 0, zero, one)
    send_ref[...] = jnp.where(core == 0, one, zero)


def gram_halves(core, count, parts, values, weight):
    out = jax.ShapeDtypeStruct((BLK // 4 + 8, BLK), F32)
    return pl.pallas_call(
        gram_kernel,
        in_specs=[pl.BlockSpec(memory_space=SMEM)] * 2 + [pl.BlockSpec(memory_space=VMEM)] * 6,
        out_specs=[pl.BlockSpec(memory_space=VMEM)] * 2,
        out_shape=[out] * 2,
        compiler_params=pltpu.CompilerParams(vmem_limit_bytes=32 * 2**20),
        name="gram",
    )(core, count, *parts, values, weight)


PANEL = 32
SLABS = PANEL // 8


def invert_factor(rows):
    sub = [lax.broadcasted_iota(jnp.int32, (8, BLK), 0) + 8 * r for r in range(SLABS)]
    lane = lax.broadcasted_iota(jnp.int32, (8, BLK), 1)
    rows = list(rows)
    done = []
    for p in range(BLK // PANEL):
        at = PANEL * p
        slab = rows[SLABS * p : SLABS * (p + 1)]
        cols = [
            [jnp.broadcast_to(part[:, at + j : at + j + 1], (8, BLK)) for part in slab] for j in range(PANEL)
        ]
        inside = (lane >= at) & (lane < at + PANEL)
        slab = [
            jnp.where(inside, jnp.where(lane - at == sub[r], 1.0, 0.0), slab[r]) for r in range(SLABS)
        ]
        result = [jnp.zeros((8, BLK), F32)] * SLABS
        for t in range(PANEL):
            first, place_in = t // 8, t % 8
            scale = lax.rsqrt(jnp.broadcast_to(cols[t][first][place_in : place_in + 1], (8, BLK)))
            factor = [None] * SLABS
            for r in range(first, SLABS):
                factor[r] = cols[t][r] * scale
            factor[first] = jnp.where(sub[first] > t, factor[first], 0.0)
            for j in range(t + 1, PANEL):
                top = jnp.broadcast_to(factor[j // 8][j % 8 : j % 8 + 1], (8, BLK))
                for r in range(j // 8, SLABS):
                    cols[j][r] = cols[j][r] - factor[r] * top
            top = jnp.broadcast_to(slab[first][place_in : place_in + 1], (8, BLK)) * scale
            result[first] = jnp.where(sub[first] == t, top, result[first])
            for r in range(first, SLABS):
                slab[r] = slab[r] - factor[r] * top
        done += [jnp.where(lane <= sub[r] + at, result[r], 0.0) for r in range(SLABS)]
        if at + PANEL < BLK:
            full = jnp.concatenate(result, axis=0)
            outer = lax.dot_general(
                full, full, (((0,), (0,)), ((), ())), precision=HIGHEST, preferred_element_type=F32
            )
            for q in range(SLABS * (p + 1), BLK // 8):
                rows[q] = jnp.where(inside, 0.0, rows[q]) - outer[8 * q : 8 * q + 8]
    return done


CHUNK = 512
CHUNKS = LEVS * CELLS // CHUNK


def analysis_kernel(
    core_ref, mine_ref, other_ref, members_hbm, out_ref, transform_ref, members_ref, result, in_sem, out_sem
):
    load = pltpu.make_async_copy(members_hbm, members_ref, in_sem)
    load.start()
    core = core_ref[0]
    mine, other = mine_ref[...], other_ref[...]
    whole, pull = unpack(jnp.where(core == 0, mine, other), jnp.where(core == 0, other, mine))
    sub = lax.broadcasted_iota(jnp.int32, (8, BLK), 0)
    lane = lax.broadcasted_iota(jnp.int32, (8, BLK), 1)
    slabs = [
        whole[8 * p : 8 * p + 8, :] + jnp.where(lane == sub + 8 * p, 1.0, 0.0) for p in range(BLK // 8)
    ]
    inverse = jnp.concatenate(invert_factor(slabs), axis=0)
    inner = jnp.sum(inverse * pull, axis=1, keepdims=True)
    shift = jnp.sum(inverse * inner, axis=0, keepdims=True)
    transform = jnp.transpose(inverse + shift * (1.0 / math.sqrt(BLK - 1)))
    transform_ref[...] = transform
    rounded = transform.astype(BF)
    average = jnp.full((BLK, BLK), 1.0 / BLK, BF)
    load.wait()
    copies = []
    for n in range(CHUNKS):
        at = slice(n * CHUNK, (n + 1) * CHUNK)
        value = members_ref[at, :]
        row_mean = jnp.dot(value, average, preferred_element_type=F32)
        anomalies = (value.astype(F32) - row_mean).astype(BF)
        moved = jnp.dot(anomalies, rounded, preferred_element_type=F32)
        result[at, :] = (row_mean + moved).astype(BF)
        copies.append(pltpu.make_async_copy(result.at[at, :], out_ref.at[at, :], out_sem.at[n]))
        copies[-1].start()
    for copy in copies:
        copy.wait()


def analysis(core, mine, other, members):
    return pl.pallas_call(
        analysis_kernel,
        in_specs=[
            pl.BlockSpec(memory_space=SMEM),
            pl.BlockSpec(memory_space=VMEM),
            pl.BlockSpec(memory_space=VMEM),
            pl.BlockSpec(memory_space=HBM),
        ],
        out_specs=[pl.BlockSpec(memory_space=HBM), pl.BlockSpec(memory_space=VMEM)],
        out_shape=[
            jax.ShapeDtypeStruct((LEVS * CELLS, BLK), BF),
            jax.ShapeDtypeStruct((BLK, BLK), F32),
        ],
        scratch_shapes=[
            pltpu.VMEM((LEVS * CELLS, BLK), BF),
            pltpu.VMEM((LEVS * CELLS, BLK), BF),
            pltpu.SemaphoreType.DMA,
            pltpu.SemaphoreType.DMA((CHUNKS,)),
        ],
        compiler_params=pltpu.CompilerParams(vmem_limit_bytes=32 * 2**20),
        name="analysis",
    )(core, mine, other, members)


def shards(members, obs_operator, col_level, col_block, obs_count, obs_values, obs_weight):
    lev = lax.axis_index("lev").astype(jnp.int32)
    core = (lev % 2).reshape(1)
    x = (lev // 2).reshape(1)
    flat = members.reshape(LEVS * CELLS, BLK)

    up = [(i, i + 1) for i in range(31)]
    down = [(i + 1, i) for i in range(31)]
    before = lax.ppermute(members[:, CELLS - RIM :], "tile", up)
    after = lax.ppermute(members[:, :RIM], "tile", down)

    places = jnp.transpose(col_level * 32 + col_block, (0, 2, 1))
    send, keep, edge, rim = inner_blocks(core, places, obs_operator, flat)
    send, before, after = lax.optimization_barrier((send, before, after))
    came = other_core(send)
    send_edge, keep_edge = outer_blocks(core, places, edge, rim, before, after)
    own, *far = pair_sum(core, x, came, keep, other_core(send_edge), keep_edge)
    parts = [own] + [x_shift(far[k - 1], k) for k in (1, 2, 3)]

    send, keep = gram_halves(core, obs_count, parts, obs_values, obs_weight)
    total = keep + other_core(send)
    total = group_sum(total, PLANES)
    total = group_sum(total, LINES)
    other = other_core(total)

    analysed, transform = analysis(core, total, other, flat)
    return (analysed.reshape(LEVS, CELLS, BLK), transform)


def solution(mesh):
    placed = (
        P("lev", "tile", None),
        P("lev", "tile", None, None, None),
        P("lev", "tile", None),
        P("lev", "tile", None),
        P(("tile", "lev")),
        P(("tile", "lev"), None),
        P(("tile", "lev"), None),
    )
    return jax.shard_map(
        shards, mesh=mesh, in_specs=placed, out_specs=(P("lev", "tile", None), P()), check_vma=False
    )
```

time: 370 us -> 85.2 us (0.23)
  waiting for transfers between devices: 209 us -> 15.3 us
  blocking collectives: 79.5 us -> 31.9 us
  other arithmetic: 28.9 us -> 0.75 us
  matrix products: 20 us -> 0 us
  Pallas kernels: 0 us -> 16.4 us
  between operations: 14.2 us -> 0.91 us
  starting transfers between devices: 5.42 us -> 16.9 us
  local copies, waits for them, and re-layouts: 12.2 us -> 2.72 us
    psum x1 -> x0, waiting for transfers between devices: 161 us -> none  [shards(): gram, pull = lax.psum((gram_local, pull_local), ('tile', 'lev'))]
    psum x1 -> x0, blocking collectives: 79.5 us -> none  [shards(): gram, pull = lax.psum((gram_local, pull_local), ('tile', 'lev'))]
    reduce_scatter x1 -> x0, waiting for transfers between devices: 41.4 us -> none  [shards(): lax.psum_scatter(jnp.einsum('okij,okjm->oim', operator_blocks, chosen, pr...]
    all_to_all x0 -> x2, blocking collectives: none -> 31.9 us  [group_sum(): lax.all_to_all(copies, ('tile', 'lev'), 0, 0, axis_index_groups=groups)]
    another operation x5 -> x0, other arithmetic: 22.9 us -> none  [the longest x3 12.4 us: shards(): lower = jnp.linalg.cholesky(identity + gram)]
    dot_general x6 -> x0, matrix products: 19.8 us -> none  [the longest x1 10.1 us: shards(): jnp.einsum('okij,okjm->oim', operator_blocks, chosen, preferred_element_t...]
    pallas_call x0 -> x5, Pallas kernels: none -> 16.4 us  [the longest x1 6.49 us: analysis(): pl.pallas_call(analysis_kernel, in_specs=[pl.BlockSpec(memory_space=SMEM)...]
    ppermute x2 -> x9, starting transfers between devices: 5.34 us -> 16.9 us  [the longest x4 7.8 us: other_core(): return lax.ppermute(value, 'lev', [(i, i ^ 1) for i in range(8)])]
  transfers between devices with their start and end apart: 4 -> 9, of which waited for: 4 -> 5; matrix products, arithmetic and copies ran while one was open for 1% -> 1% of each run, Pallas kernels for 0% -> 9%
where the time goes in v1:
time: 85.2 us; the launch traced here: 84.9 us
  blocking collectives  31.9 us (37%)
  starting transfers between devices  16.9 us (20%)
  Pallas kernels  16.4 us (19%)
  waiting for transfers between devices  15.3 us (18%)
  local copies, waits for them, and re-layouts  2.72 us (3%)
  between operations  0.91 us (1%)
    all_to_all x2, blocking collectives, group_sum(): lax.all_to_all(copies, ('tile', 'lev'), 0, 0, axis_index_groups=groups)  31.9 us
    ppermute x3, waiting for transfers between devices, x_shift(): lax.ppermute(value, 'lev', [(i, (i + 2 * step) % 8) for i in range(8)])  12.2 us
    ppermute x4, starting transfers between devices, other_core(): return lax.ppermute(value, 'lev', [(i, i ^ 1) for i in range(8)])  7.8 us
    pallas_call x1, Pallas kernels, analysis(): pl.pallas_call(analysis_kernel, in_specs=[pl.BlockSpec(memory_space=SMEM)...  6.49 us
    pallas_call x1, Pallas kernels, inner_blocks(): pl.pallas_call(inner_kernel, in_specs=[pl.BlockSpec(memory_space=SMEM)] *...  6.3 us
    ppermute x1, starting transfers between devices, shards(): before = lax.ppermute(members[:, CELLS - RIM:], 'tile', up)  4.67 us
    ppermute x4, waiting for transfers between devices, other_core(): return lax.ppermute(value, 'lev', [(i, i ^ 1) for i in range(8)])  3.19 us
    ppermute x3, starting transfers between devices, x_shift(): lax.ppermute(value, 'lev', [(i, (i + 2 * step) % 8) for i in range(8)])  3.15 us
  transfers between devices with their start and end apart: 9, of which 5 were waited for; matrix products, arithmetic and copies ran while one was open for 1% of the time, Pallas kernels for 9%

profile of v1, /device:TPU:1, one launch (start us, length us, event | category | flops | bytes accessed | tf_op | source)
XLA Modules:
  0.0 84.9 jit_solution(1700382278328537248)
XLA Ops:
  0.6 1.1 %fusion = (bf16[4,256,128]{2,1,0:T(8,128)(2,1)S(1)}, bf16[4,256,128]{2,1,0:T(8,128)(2,1)S(1)}) fusion(bf16[4,2048,128]{2,1,0:T(8,128)(2,1)} %param.7), kind=kLoop, calls=%fused_computation.1 | loop fusion | bytes 1048576 | tf_op jit(solution)/shard_map/slice | solution.py:432
  1.7 1.3 %collective-permute-start.1 = (bf16[4,256,128]{2,1,0:T(8,128)(2,1)S(1)}, bf16[4,256,128]{2,1,0:T(8,128)(2,1)S(1)}, u32[]{:S(2)}, u32[]{:S(2)}) collective-permute-start(bf16[4,256,128]{2,1,0:T(8,128)(2,1)S(1)} %get-tuple-element.36), channel_id=1, source_target_pairs={{8,0},{16,8},{24,16},{32,24},{40,32},{48,40},{56,48},{64,56},{72,6... | collective-permute-start | bytes 786440 | tf_op jit(solution)/shard_map/ppermute | solution.py:432
  3.0 4.7 %collective-permute-start = (bf16[4,256,128]{2,1,0:T(8,128)(2,1)S(1)}, bf16[4,256,128]{2,1,0:T(8,128)(2,1)S(1)}, u32[]{:S(2)}, u32[]{:S(2)}) collective-permute-start(bf16[4,256,128]{2,1,0:T(8,128)(2,1)S(1)} %get-tuple-element.37), channel_id=1, source_target_pairs={{0,8},{8,16},{16,24},{24,32},{32,40},{40,48},{48,56},{56,64},{64,7... | collective-permute-start | bytes 786440 | tf_op jit(solution)/shard_map/ppermute | solution.py:431
  7.7 0.7 add_bitcast_fusion.at_ref
  8.4 1.6 %copy-done = bf16[4,2048,128]{2,1,0:T(8,128)(2,1)S(1)} copy-done((bf16[4,2048,128]{2,1,0:T(8,128)(2,1)S(1)}, bf16[4,2048,128]{2,1,0:T(8,128)(2,1)}, u32[]{:S(2)}) %copy-start) | copy-done | bytes 2097176
  10.0 6.3 %observe_inner.1 = (bf16[3,1056,128]{2,1,0:T(8,128)(2,1)S(1)}, bf16[3,1056,128]{2,1,0:T(8,128)(2,1)S(1)}, bf16[2,1,8,4,128,128]{5,4,3,2,1,0:T(8,128)(2,1)S(1)}, bf16[2,4,512,128]{3,2,1,0:T(8,128)(2,1)S(1)}) custom-call(s32[1]{0:T(128)} %bitcast.core_ref, s32[1,4,64]{2,1,0:T(4,128)S(1)} %add_bitcast_fusion.at_ref, bf16[1,64,4,128,128]{4,3,2,1,0:T(8,128)(2,1)} %op_hbm.1, ...), custom_call_target="tpu_custom_call" | custom-call | flops 1000000 | bytes 65536 | tf_op jit(solution)/shard_map/observe_inner/pallas_call | solution.py:134
  16.3 3.2 %collective-permute-start.2 = (bf16[3,1056,128]{2,1,0:T(8,128)(2,1)S(1)}, bf16[3,1056,128]{2,1,0:T(8,128)(2,1)S(1)}, u32[]{:S(2)}, u32[]{:S(2)}) collective-permute-start(bf16[3,1056,128]{2,1,0:T(8,128)(2,1)S(1)} %get-tuple-element.20), channel_id=1, source_target_pairs={{0,1},{1,0},{2,3},{3,2},{4,5},{5,4},{6,7},{7,6},{8,9},{9,8},{10,11... | collective-permute-start | bytes 2433032 | tf_op jit(solution)/shard_map/ppermute | solution.py:31
  19.5 1.6 %observe_outer.1 = (bf16[1056,128]{1,0:T(8,128)(2,1)S(1)}, bf16[1056,128]{1,0:T(8,128)(2,1)S(1)}) custom-call(s32[1]{0:T(128)} %bitcast.core_ref, s32[1,4,64]{2,1,0:T(4,128)S(1)} %add_bitcast_fusion.at_ref, bf16[2,1,8,4,128,128]{5,4,3,2,1,0:T(8,128)(2,1)S(1)} %get-tuple-element.22.edge_ref, bf16[2,4,512,128]{3,2,1,0:T(8,128)(2,1)S(1)} %get-tuple-element.23.rim_ref, ...), custom_call_target="tpu_custom_call" | custom-call | flops 270000000 | bytes 4194304 | tf_op jit(solution)/shard_map/observe_outer/pallas_call | solution.py:182
  21.2 0.1 collective-permute-start.3
  21.3 1.5 %collective-permute-done.3.came_edge = bf16[1056,128]{1,0:T(8,128)(2,1)S(1)} collective-permute-done((bf16[1056,128]{1,0:T(8,128)(2,1)S(1)}, bf16[1056,128]{1,0:T(8,128)(2,1)S(1)}, u32[]{:S(2)}, u32[]{:S(2)}) %collective-permute-start.3) | collective-permute-done | bytes 270368 | tf_op jit(solution)/shard_map/ppermute | solution.py:31
  22.8 0.3 pair_sum.1
  23.1 0.1 collective-permute-start.4
  23.2 1.9 %collective-permute-start.5 = (bf16[1056,128]{1,0:T(8,128)(2,1)S(1)}, bf16[1056,128]{1,0:T(8,128)(2,1)S(1)}, u32[]{:S(2)}, u32[]{:S(2)}) collective-permute-start(bf16[1056,128]{1,0:T(8,128)(2,1)S(1)} %get-tuple-element.30), channel_id=1, source_target_pairs={{0,4},{1,5},{2,6},{3,7},{4,0},{5,1},{6,2},{7,3},{8,12},{9,13},{10,... | collective-permute-start | bytes 811016 | tf_op jit(solution)/shard_map/ppermute | solution.py:35
  25.1 1.1 %collective-permute-start.6 = (bf16[1056,128]{1,0:T(8,128)(2,1)S(1)}, bf16[1056,128]{1,0:T(8,128)(2,1)S(1)}, u32[]{:S(2)}, u32[]{:S(2)}) collective-permute-start(bf16[1056,128]{1,0:T(8,128)(2,1)S(1)} %get-tuple-element.31), channel_id=1, source_target_pairs={{0,6},{1,7},{2,0},{3,1},{4,2},{5,3},{6,4},{7,5},{8,14},{9,15},{10,... | collective-permute-start | bytes 811016 | tf_op jit(solution)/shard_map/ppermute | solution.py:35
  26.3 11.9 %collective-permute-done.4.b_ref = bf16[1056,128]{1,0:T(8,128)(2,1)S(1)} collective-permute-done((bf16[1056,128]{1,0:T(8,128)(2,1)S(1)}, bf16[1056,128]{1,0:T(8,128)(2,1)S(1)}, u32[]{:S(2)}, u32[]{:S(2)}) %collective-permute-start.4) | collective-permute-done | bytes 270368 | tf_op jit(solution)/shard_map/ppermute | solution.py:35
  38.1 0.3 collective-permute-done.6.d_ref
  38.4 1.7 %gram.1 = (f32[40,128]{1,0:T(8,128)S(1)}, f32[40,128]{1,0:T(8,128)S(1)}) custom-call(s32[1]{0:T(128)} %bitcast.core_ref, s32[8]{0:T(128)S(1)} %copy-done.4, bf16[1056,128]{1,0:T(8,128)(2,1)S(1)} %get-tuple-element.28.a_ref, bf16[1056,128]{1,0:T(8,128)(2,1)S(1)} %collective-permute-done.4.b_ref, bf16[1056,128]{1,0:T(8,128)(2,1)S(1)} %collective-permute-done.5.c_ref, ...), custom_call_target="tpu_custom_call" | custom-call | tf_op jit(solution)/shard_map/gram/pallas_call | solution.py:303
  40.1 1.3 %collective-permute-start.7 = (f32[40,128]{1,0:T(8,128)S(1)}, f32[40,128]{1,0:T(8,128)S(1)}, u32[]{:S(2)}, u32[]{:S(2)}) collective-permute-start(f32[40,128]{1,0:T(8,128)S(1)} %get-tuple-element.33), channel_id=1, source_target_pairs={{0,1},{1,0},{2,3},{3,2},{4,5},{5,4},{6,7},{7,6},{8,9},{9,8},{10,11... | collective-permute-start | bytes 61448 | tf_op jit(solution)/shard_map/ppermute | solution.py:31
  41.4 0.8 collective-permute-done.7
  42.3 15.6 %all_to_all.10 = f32[16,40,128]{2,1,0:T(8,128)S(1)} all-to-all(f32[16,40,128]{2,1,0:T(8,128)S(1)} %broadcast_in_dim.4), channel_id=1, replica_groups={{0,2,4,6,8,10,12,14,16,18,20,22,24,26,28,30},{1,3,5,7,9,11,13,15,17,19,..., dimensions={0} | all-to-all | bytes 655360 | tf_op jit(solution)/shard_map/all_to_all | solution.py:48
  57.9 16.3 %all_to_all.11 = f32[8,40,128]{2,1,0:T(8,128)S(1)} all-to-all(f32[8,40,128]{2,1,0:T(8,128)S(1)} %broadcast_in_dim.5), channel_id=1, replica_groups={{0,32,64,96,128,160,192,224},{1,33,65,97,129,161,193,225},{2,34,66,98,1..., dimensions={0} | all-to-all | bytes 327680 | tf_op jit(solution)/shard_map/all_to_all | solution.py:48
  74.3 3.1 %collective-permute-start.8 = (f32[40,128]{1,0:T(8,128)S(1)}, f32[40,128]{1,0:T(8,128)S(1)}, u32[]{:S(2)}, u32[]{:S(2)}) collective-permute-start(f32[40,128]{1,0:T(8,128)S(1)} %reduce_sum.19.mine_ref), channel_id=1, source_target_pairs={{0,1},{1,0},{2,3},{3,2},{4,5},{5,4},{6,7},{7,6},{8,9},{9,8},{10,11... | collective-permute-start | bytes 61448 | tf_op jit(solution)/shard_map/ppermute | solution.py:31
  77.4 0.8 collective-permute-done.8.other_ref
  78.2 6.5 %analysis.1 = (bf16[8192,128]{1,0:T(8,128)(2,1)}, f32[128,128]{1,0:T(8,128)}) custom-call(s32[1]{0:T(128)} %bitcast.core_ref, f32[40,128]{1,0:T(8,128)S(1)} %reduce_sum.19.mine_ref, f32[40,128]{1,0:T(8,128)S(1)} %collective-permute-done.8.other_ref, bf16[8192,128]{1,0:T(8,128)(2,1)S(1)} %bitcast.7), custom_call_target="tpu_custom_call" | custom-call | tf_op jit(solution)/shard_map/analysis/pallas_call | solution.py:399
  (18 shorter events, 0.1 us)
Async XLA Ops:
  1.7 14.6 %collective-permute-start.1 = (bf16[4,256,128]{2,1,0:T(8,128)(2,1)S(1)}, bf16[4,256,128]{2,1,0:T(8,128)(2,1)S(1)}, u32[]{:S(2)}, u32[]{:S(2)}) collective-permute-start(bf16[4,256,128]{2,1,0:T(8,128)(2,1)S(1)} %get-tuple-element.36), channel_id=1, source_target_pairs={{8,0},{16,8},{24,16},{32,24},{40,32},{48,40},{56,48},{64,56},{72,6... | collective-permute-start | bytes 786440 | tf_op jit(solution)/shard_map/ppermute | solution.py:432
  3.0 13.3 %collective-permute-start = (bf16[4,256,128]{2,1,0:T(8,128)(2,1)S(1)}, bf16[4,256,128]{2,1,0:T(8,128)(2,1)S(1)}, u32[]{:S(2)}, u32[]{:S(2)}) collective-permute-start(bf16[4,256,128]{2,1,0:T(8,128)(2,1)S(1)} %get-tuple-element.37), channel_id=1, source_target_pairs={{0,8},{8,16},{16,24},{24,32},{32,40},{40,48},{48,56},{56,64},{64,7... | collective-permute-start | bytes 786440 | tf_op jit(solution)/shard_map/ppermute | solution.py:431
  8.4 1.6 %copy-start = (bf16[4,2048,128]{2,1,0:T(8,128)(2,1)S(1)}, bf16[4,2048,128]{2,1,0:T(8,128)(2,1)}, u32[]{:S(2)}) copy-start(bf16[4,2048,128]{2,1,0:T(8,128)(2,1)} %param.7) | copy-start | bytes 6291460
  16.3 6.4 %collective-permute-start.2 = (bf16[3,1056,128]{2,1,0:T(8,128)(2,1)S(1)}, bf16[3,1056,128]{2,1,0:T(8,128)(2,1)S(1)}, u32[]{:S(2)}, u32[]{:S(2)}) collective-permute-start(bf16[3,1056,128]{2,1,0:T(8,128)(2,1)S(1)} %get-tuple-element.20), channel_id=1, source_target_pairs={{0,1},{1,0},{2,3},{3,2},{4,5},{5,4},{6,7},{7,6},{8,9},{9,8},{10,11... | collective-permute-start | bytes 2433032 | tf_op jit(solution)/shard_map/ppermute | solution.py:31
  19.5 18.9 %copy-start.2 = (f32[8,128]{1,0:T(8,128)S(1)}, f32[8,128]{1,0:T(8,128)}, u32[]{:S(2)}) copy-start(f32[8,128]{1,0:T(8,128)} %values_ref.1) | copy-start | bytes 12292
  19.5 18.9 %copy-start.3 = (f32[8,128]{1,0:T(8,128)S(1)}, f32[8,128]{1,0:T(8,128)}, u32[]{:S(2)}) copy-start(f32[8,128]{1,0:T(8,128)} %weight_ref.1) | copy-start | bytes 12292
  19.5 18.9 %copy-start.4 = (s32[8]{0:T(128)S(1)}, s32[8]{0:T(128)}, u32[]{:S(2)}) copy-start(s32[8]{0:T(128)} %count_ref.1) | copy-start | bytes 100
  21.2 1.6 %collective-permute-start.3 = (bf16[1056,128]{1,0:T(8,128)(2,1)S(1)}, bf16[1056,128]{1,0:T(8,128)(2,1)S(1)}, u32[]{:S(2)}, u32[]{:S(2)}) collective-permute-start(bf16[1056,128]{1,0:T(8,128)(2,1)S(1)} %get-tuple-element.26), channel_id=1, source_target_pairs={{0,1},{1,0},{2,3},{3,2},{4,5},{5,4},{6,7},{7,6},{8,9},{9,8},{10,11... | collective-permute-start | bytes 811016 | tf_op jit(solution)/shard_map/ppermute | solution.py:31
  23.1 55.2 %copy-start.1 = (bf16[4,2048,128]{2,1,0:T(8,128)(2,1)S(1)}, bf16[4,2048,128]{2,1,0:T(8,128)(2,1)}, u32[]{:S(2)}) copy-start(bf16[4,2048,128]{2,1,0:T(8,128)(2,1)} %param.7) | copy-start | bytes 6291460
  23.1 15.0 %collective-permute-start.4 = (bf16[1056,128]{1,0:T(8,128)(2,1)S(1)}, bf16[1056,128]{1,0:T(8,128)(2,1)S(1)}, u32[]{:S(2)}, u32[]{:S(2)}) collective-permute-start(bf16[1056,128]{1,0:T(8,128)(2,1)S(1)} %get-tuple-element.29), channel_id=1, source_target_pairs={{0,2},{1,3},{2,4},{3,5},{4,6},{5,7},{6,0},{7,1},{8,10},{9,11},{10,... | collective-permute-start | bytes 811016 | tf_op jit(solution)/shard_map/ppermute | solution.py:35
  23.2 14.9 %collective-permute-start.5 = (bf16[1056,128]{1,0:T(8,128)(2,1)S(1)}, bf16[1056,128]{1,0:T(8,128)(2,1)S(1)}, u32[]{:S(2)}, u32[]{:S(2)}) collective-permute-start(bf16[1056,128]{1,0:T(8,128)(2,1)S(1)} %get-tuple-element.30), channel_id=1, source_target_pairs={{0,4},{1,5},{2,6},{3,7},{4,0},{5,1},{6,2},{7,3},{8,12},{9,13},{10,... | collective-permute-start | bytes 811016 | tf_op jit(solution)/shard_map/ppermute | solution.py:35
  25.1 13.3 %collective-permute-start.6 = (bf16[1056,128]{1,0:T(8,128)(2,1)S(1)}, bf16[1056,128]{1,0:T(8,128)(2,1)S(1)}, u32[]{:S(2)}, u32[]{:S(2)}) collective-permute-start(bf16[1056,128]{1,0:T(8,128)(2,1)S(1)} %get-tuple-element.31), channel_id=1, source_target_pairs={{0,6},{1,7},{2,0},{3,1},{4,2},{5,3},{6,4},{7,5},{8,14},{9,15},{10,... | collective-permute-start | bytes 811016 | tf_op jit(solution)/shard_map/ppermute | solution.py:35
  40.1 2.2 %collective-permute-start.7 = (f32[40,128]{1,0:T(8,128)S(1)}, f32[40,128]{1,0:T(8,128)S(1)}, u32[]{:S(2)}, u32[]{:S(2)}) collective-permute-start(f32[40,128]{1,0:T(8,128)S(1)} %get-tuple-element.33), channel_id=1, source_target_pairs={{0,1},{1,0},{2,3},{3,2},{4,5},{5,4},{6,7},{7,6},{8,9},{9,8},{10,11... | collective-permute-start | bytes 61448 | tf_op jit(solution)/shard_map/ppermute | solution.py:31
  74.3 4.0 %collective-permute-start.8 = (f32[40,128]{1,0:T(8,128)S(1)}, f32[40,128]{1,0:T(8,128)S(1)}, u32[]{:S(2)}, u32[]{:S(2)}) collective-permute-start(f32[40,128]{1,0:T(8,128)S(1)} %reduce_sum.19.mine_ref), channel_id=1, source_target_pairs={{0,1},{1,0},{2,3},{3,2},{4,5},{5,4},{6,7},{7,6},{8,9},{9,8},{10,11... | collective-permute-start | bytes 61448 | tf_op jit(solution)/shard_map/ppermute | solution.py:31
